TPU v7x, 256 devices: a whole 4x4x8 slice. The times are simulated.
256 devices in a mesh: pair: 64 (over y, z, x_hi), row: 4 (over x_lo, core).
Axes of the slice: x: 4 (x_hi: 2, x_lo: 2; x = x_hi * 2 + x_lo), y: 4, z: 8, core: 2. Of those that a mesh axis runs over, the one named last changes fastest.
Arguments:
- matrix: float32 [8192, 16384], P('row', 'pair'), may hold values from -8.75 to 8.75
- vectors: float32 [4096, 16384], P('row', 'pair'), may hold values from -6 to 6
Outputs:
- matrix_out: float32 [8192, 16384], P('row', 'pair')
- vectors_out: float32 [4096, 16384], P('row', 'pair')
- off_mass: float32 [2], replicated
All inputs are finite; a program needn't handle non-finite values.
Results may differ from a plain program's by a relative error of at most 0.00021.
Values sent between devices are 32-bit elements; how exact they have to be, the bound alone decides.
A program may use at most 64 MiB of HBM per device.

v0:
```python
import jax
import jax.numpy as jnp
from jax import lax
from jax.sharding import PartitionSpec as P

ORTH = 2


HIGH = lax.Precision.HIGHEST


def shifted(value, axis, steps):
    count = lax.axis_size(axis)
    initial, last = (max(0, -steps), min(count, count - steps))
    return lax.ppermute(value, axis, [(source, source + steps) for source in range(initial, last)])


def rotation(gram_matrix):
    current = gram_matrix
    rotated = gram_matrix
    for iteration in range(ORTH):
        product = jnp.dot(current.T, current, precision=HIGH)
        factor = jnp.linalg.cholesky(product)
        rotated = lax.linalg.triangular_solve(
            factor, current, left_side=False, lower=True, transpose_a=True
        )
        if iteration + 1 < ORTH:
            current = jnp.dot(gram_matrix, rotated, precision=HIGH)
    return rotated


def off_term(gram_matrix):
    outside = 1.0 - jnp.eye(gram_matrix.shape[0], dtype=jnp.float32)
    return jnp.sum(gram_matrix * gram_matrix * outside)


def slot_gram(pair_block):
    partial_gram = jnp.dot(pair_block.T, pair_block, precision=HIGH)
    return lax.psum(partial_gram, "row")


def round_tally(gram_matrix):
    return lax.psum(off_term(gram_matrix), "pair")


def local(matrix, vectors):
    half = matrix.shape[1] // 2
    rows_a = matrix.shape[0]
    position = lax.axis_index("pair")
    first = position == 0
    final = position == lax.axis_size("pair") - 1
    total_rows = float(rows_a * lax.axis_size("row"))
    scale = 1.0 / (total_rows * total_rows * float(lax.axis_size("pair")))
    gram_one = slot_gram(matrix)
    turn_one = rotation(gram_one)
    matrix_one = jnp.dot(matrix, turn_one, precision=HIGH)
    top_a = matrix_one[:, :half]
    bottom_a = matrix_one[:, half:]
    send_a = jnp.where(first, bottom_a, top_a)
    vectors_one = jnp.dot(vectors, turn_one, precision=HIGH)
    top_v = vectors_one[:, :half]
    bottom_v = vectors_one[:, half:]
    send_v = jnp.where(first, bottom_v, top_v)
    arrived_up = shifted(jnp.concatenate([send_a, send_v], axis=0), "pair", 1)
    arrived_down = shifted(jnp.concatenate([bottom_a, bottom_v], axis=0), "pair", -1)
    moved_top_v = jnp.where(first, top_v, arrived_up[rows_a:])
    moved_bottom_v = jnp.where(final, top_v, arrived_down[rows_a:])
    new_top = jnp.where(first, top_a, arrived_up[:rows_a])
    new_bottom = jnp.where(final, top_a, arrived_down[:rows_a])
    matrix_two = jnp.concatenate([new_top, new_bottom], axis=1)
    gram_two = slot_gram(matrix_two)
    turn_two = rotation(gram_two)
    matrix_out = jnp.dot(matrix_two, turn_two, precision=HIGH)
    vectors_out = jnp.dot(
        jnp.concatenate([moved_top_v, moved_bottom_v], axis=1), turn_two, precision=HIGH
    )
    masses = jnp.stack([round_tally(gram_one), round_tally(gram_two)])
    off_mass = masses * scale
    return (matrix_out, vectors_out, off_mass)


def solution(mesh):
    return jax.shard_map(
        local,
        mesh=mesh,
        in_specs=(P("row", "pair"), P("row", "pair")),
        out_specs=(P("row", "pair"), P("row", "pair"), P()),
        check_vma=False,
    )
```

profile of v0, /device:TPU:2, one launch (start us, length us, event | category | flops | bytes accessed | tf_op | source)
XLA Modules:
  0.0 638.5 jit_solution(9306734840323191330)
XLA Ops:
  8.8 4.2 fusion.62
  13.2 43.1 %all-reduce.5.cloned.1.call-done = f32[256,256]{1,0:T(8,128)} async-done(((f32[256,256]{1,0:T(8,128)}), f32[256,256]{1,0:T(8,128)}) %all-reduce.5.cloned.1.call-update) | async-done | bytes 262160 | tf_op jit(solution)/shard_map/psum | solution.py:39
  58.2 11.7 %cholesky.214 = f32[128,128]{1,0:T(8,128)S(1)} custom-call(f32[128,128]{1,0:T(8,128)S(1)} %cholesky.346), custom_call_target="Cholesky" | custom-call | tf_op jit(solution)/shard_map/jit(cholesky)/cholesky | solution.py:23
  69.9 9.8 %custom-call.17 = f32[1,128,128]{1,2,0:T(8,128)S(1)} custom-call(f32[1,128,128]{2,1,0:T(8,128)S(1)} %get-tuple-element.100), custom_call_target="InvertDiagBlocksLowerTriangular" | custom-call | tf_op jit(solution)/shard_map/jit(cholesky)/cholesky | solution.py:23
  80.2 11.7 %cholesky.231 = f32[128,128]{1,0:T(8,128)S(1)} custom-call(f32[128,128]{1,0:T(8,128)S(1)} %convolution_subtract_fusion.6), custom_call_target="Cholesky" | custom-call | tf_op jit(solution)/shard_map/jit(cholesky)/cholesky | solution.py:23
  94.1 4.0 while.8
  98.1 20.1 %custom-call.18 = f32[2,128,128]{1,2,0:T(8,128)S(1)} custom-call(f32[2,128,128]{2,1,0:T(8,128)S(1)} %get-tuple-element.31), custom_call_target="InvertDiagBlocksLowerTriangular" | custom-call | tf_op jit(solution)/shard_map/triangular_solve/custom-call.0 | solution.py:24
  120.4 11.7 %cholesky.248 = f32[128,128]{1,0:T(8,128)S(1)} custom-call(f32[128,128]{1,0:T(8,128)S(1)} %cholesky.349), custom_call_target="Cholesky" | custom-call | tf_op jit(solution)/shard_map/jit(cholesky)/cholesky | solution.py:23
  132.2 9.8 %custom-call.19 = f32[1,128,128]{1,2,0:T(8,128)S(1)} custom-call(f32[1,128,128]{2,1,0:T(8,128)S(1)} %get-tuple-element.96), custom_call_target="InvertDiagBlocksLowerTriangular" | custom-call | tf_op jit(solution)/shard_map/jit(cholesky)/cholesky | solution.py:23
  142.5 11.7 %cholesky.265 = f32[128,128]{1,0:T(8,128)S(1)} custom-call(f32[128,128]{1,0:T(8,128)S(1)} %convolution_subtract_fusion.5), custom_call_target="Cholesky" | custom-call | tf_op jit(solution)/shard_map/jit(cholesky)/cholesky | solution.py:23
  156.9 4.2 while.9
  161.1 19.7 %custom-call.20 = f32[2,128,128]{1,2,0:T(8,128)S(1)} custom-call(f32[2,128,128]{2,1,0:T(8,128)S(1)} %get-tuple-element.32), custom_call_target="InvertDiagBlocksLowerTriangular" | custom-call | tf_op jit(solution)/shard_map/triangular_solve/custom-call.0 | solution.py:24
  181.8 1.9 convolution_bitcast_fusion
  189.0 7.2 %collective-permute-start = (f32[3072,128]{0,1:T(8,128)}, f32[3072,128]{0,1:T(8,128)}, u32[]{:S(2)}, u32[]{:S(2)}) collective-permute-start(f32[3072,128]{0,1:T(8,128)} %pad_maximum_fusion.3), channel_id=1, source_target_pairs={{0,4},{4,8},{8,12},{12,16},{16,20},{20,24},{24,28},{28,32},{32,36}... | collective-permute-start | bytes 4718600 | tf_op jit(solution)/shard_map/ppermute | solution.py:15
  196.9 64.0 %collective-permute-done.1 = f32[3072,128]{0,1:T(8,128)} collective-permute-done((f32[3072,128]{0,1:T(8,128)}, f32[3072,128]{0,1:T(8,128)}, u32[]{:S(2)}, u32[]{:S(2)}) %collective-permute-start.1) | collective-permute-done | bytes 1572896 | tf_op jit(solution)/shard_map/ppermute | solution.py:15
  260.8 2.0 slice_select_fusion.1
  264.2 2.6 fusion.1
  266.8 2.3 slice_select_fusion.4
  269.1 40.5 %all-reduce.7.cloned.1.call-done = f32[256,256]{1,0:T(8,128)} async-done(((f32[256,256]{1,0:T(8,128)}), f32[256,256]{1,0:T(8,128)}) %all-reduce.7.cloned.1.call-update) | async-done | bytes 262160 | tf_op jit(solution)/shard_map/psum | solution.py:39
  311.5 11.7 %cholesky.282 = f32[128,128]{1,0:T(8,128)S(1)} custom-call(f32[128,128]{1,0:T(8,128)S(1)} %cholesky.352), custom_call_target="Cholesky" | custom-call | tf_op jit(solution)/shard_map/jit(cholesky)/cholesky | solution.py:23
  323.3 9.8 %custom-call.21 = f32[1,128,128]{1,2,0:T(8,128)S(1)} custom-call(f32[1,128,128]{2,1,0:T(8,128)S(1)} %get-tuple-element.92), custom_call_target="InvertDiagBlocksLowerTriangular" | custom-call | tf_op jit(solution)/shard_map/jit(cholesky)/cholesky | solution.py:23
  333.6 12.1 %cholesky.299 = f32[128,128]{1,0:T(8,128)S(1)} custom-call(f32[128,128]{1,0:T(8,128)S(1)} %convolution_subtract_fusion.4), custom_call_target="Cholesky" | custom-call | tf_op jit(solution)/shard_map/jit(cholesky)/cholesky | solution.py:23
  348.2 3.8 while.10
  352.0 19.7 %custom-call.22 = f32[2,128,128]{1,2,0:T(8,128)S(1)} custom-call(f32[2,128,128]{2,1,0:T(8,128)S(1)} %get-tuple-element.33), custom_call_target="InvertDiagBlocksLowerTriangular" | custom-call | tf_op jit(solution)/shard_map/triangular_solve/custom-call.0 | solution.py:24
  373.9 11.7 %cholesky.316 = f32[128,128]{1,0:T(8,128)S(1)} custom-call(f32[128,128]{1,0:T(8,128)S(1)} %cholesky.355), custom_call_target="Cholesky" | custom-call | tf_op jit(solution)/shard_map/jit(cholesky)/cholesky | solution.py:23
  385.7 9.8 %custom-call.23 = f32[1,128,128]{1,2,0:T(8,128)S(1)} custom-call(f32[1,128,128]{2,1,0:T(8,128)S(1)} %get-tuple-element.88), custom_call_target="InvertDiagBlocksLowerTriangular" | custom-call | tf_op jit(solution)/shard_map/jit(cholesky)/cholesky | solution.py:23
  396.0 11.7 %cholesky.333 = f32[128,128]{1,0:T(8,128)S(1)} custom-call(f32[128,128]{1,0:T(8,128)S(1)} %convolution_subtract_fusion.3), custom_call_target="Cholesky" | custom-call | tf_op jit(solution)/shard_map/jit(cholesky)/cholesky | solution.py:23
  410.4 4.2 while.11
  414.6 19.7 %custom-call.24 = f32[2,128,128]{1,2,0:T(8,128)S(1)} custom-call(f32[2,128,128]{2,1,0:T(8,128)S(1)} %get-tuple-element.34), custom_call_target="InvertDiagBlocksLowerTriangular" | custom-call | tf_op jit(solution)/shard_map/triangular_solve/custom-call.0 | solution.py:24
  436.0 184.4 %all-reduce.1 = (f32[1]{0:T(128)}, f32[1]{0:T(128)}) all-reduce(f32[1]{0:T(128)} %bitcast.27, f32[1]{0:T(128)} %bitcast.26), channel_id=1, replica_groups=mesh['pair'=64,'row'=4] {'pair'}, use_global_device_ids=true, to_apply=%region_9.12 | all-reduce | flops 2 | bytes 16 | tf_op jit(solution)/shard_map/psum | solution.py:43
  622.2 6.4 %fusion = f32[2048,256]{1,0:T(8,128)} fusion(f32[2048,128]{0,1:T(8,128)} %copy-done.5, f32[2048,128]{0,1:T(8,128)} %copy-done.4, f32[256,128]{0,1:T(8,128)S(1)} %fusion.27, f32[256,128]{0,1:T(8,128)S(1)} %bitcast.147), kind=kOutput, calls=%fused_computation.10 | convolution fusion | flops 1611202560 | bytes 4456448 | tf_op jit(solution)/shard_map/dot_general | solution.py:73
  628.6 2.8 fusion.2
  (123 shorter events, 44.1 us)
Async XLA Ops:
  7.2 1.6 copy-start
  7.2 49.2 %all-reduce.5.cloned.1.call-start = ((), (), s32[]{:S(2)}) async-start(), calls=%async_computation | async-start | bytes 524288 | tf_op jit(solution)/shard_map/psum | solution.py:39
  13.0 296.6 %all-reduce.7.cloned.1.call-start = ((), (), s32[]{:S(2)}) async-start(), calls=%async_computation.1 | async-start | bytes 524288 | tf_op jit(solution)/shard_map/psum | solution.py:39
  58.0 60.2 %copy-start.2 = (f32[256,256]{1,0:T(8,128)S(1)}, f32[256,256]{1,0:T(8,128)}, u32[]{:S(2)}) copy-start(f32[256,256]{1,0:T(8,128)} %all-reduce.5.cloned.1.call-done) | copy-start | bytes 786436
  181.8 2.0 copy-start.8
  183.7 1.3 copy-start.1
  186.4 74.4 %collective-permute-start.1 = (f32[3072,128]{0,1:T(8,128)}, f32[3072,128]{0,1:T(8,128)}, u32[]{:S(2)}, u32[]{:S(2)}) collective-permute-start(f32[3072,128]{0,1:T(8,128)} %pad_maximum_fusion.4), channel_id=1, source_target_pairs={{4,0},{8,4},{12,8},{16,12},{20,16},{24,20},{28,24},{32,28},{36,32}... | collective-permute-start | bytes 4718600 | tf_op jit(solution)/shard_map/ppermute | solution.py:15
  189.0 71.8 %collective-permute-start = (f32[3072,128]{0,1:T(8,128)}, f32[3072,128]{0,1:T(8,128)}, u32[]{:S(2)}, u32[]{:S(2)}) collective-permute-start(f32[3072,128]{0,1:T(8,128)} %pad_maximum_fusion.3), channel_id=1, source_target_pairs={{0,4},{4,8},{8,12},{12,16},{16,20},{20,24},{24,28},{28,32},{32,36}... | collective-permute-start | bytes 4718600 | tf_op jit(solution)/shard_map/ppermute | solution.py:15
  262.9 1.0 copy-start.4
  262.9 1.3 copy-start.5
  311.3 60.4 %copy-start.3 = (f32[256,256]{1,0:T(8,128)S(1)}, f32[256,256]{1,0:T(8,128)}, u32[]{:S(2)}) copy-start(f32[256,256]{1,0:T(8,128)} %all-reduce.7.cloned.1.call-done) | copy-start | bytes 786436
  622.2 6.4 %copy-start.6 = (f32[1024,128]{0,1:T(8,128)S(1)}, f32[1024,128]{0,1:T(8,128)}, u32[]{:S(2)}) copy-start(f32[1024,128]{0,1:T(8,128)} %get-tuple-element.81) | copy-start | bytes 1572868
  622.2 6.4 %copy-start.7 = (f32[1024,128]{0,1:T(8,128)S(1)}, f32[1024,128]{0,1:T(8,128)}, u32[]{:S(2)}) copy-start(f32[1024,128]{0,1:T(8,128)} %get-tuple-element.82) | copy-start | bytes 1572868
Sparse Core Ops, SparseCore 0:
  13.1 43.2 all-reduce.4
  266.9 42.6 all-reduce.6
where the time goes:
time: 642 us; the launch traced here: 638 us
  other arithmetic  228 us (36%)
  blocking collectives  184 us (29%)
  waiting for transfers between devices  148 us (23%)
  matrix products  30.2 us (5%)
  between operations  19.9 us (3%)
  local copies, waits for them, and re-layouts  19.2 us (3%)
  starting transfers between devices  8.73 us (1%)
    psum x1, blocking collectives, round_tally(): return lax.psum(off_term(gram_matrix), 'pair')  184 us
    another operation x27, other arithmetic, rotation(): factor = jnp.linalg.cholesky(product)  138 us
    psum x2, waiting for transfers between devices, slot_gram(): return lax.psum(partial_gram, 'row')  83.6 us
    another operation x9, other arithmetic, rotation(): lax.linalg.triangular_solve(factor, current, left_side=False, lower=True,...  79.2 us
    ppermute x2, waiting for transfers between devices, shifted(): lax.ppermute(value, axis, [(source, source + steps) for source in range(i...  64 us
    another operation x29, local copies, waits for them, and re-layouts, rotation(): lax.linalg.triangular_solve(factor, current, left_side=False, lower=True,...  15.7 us
  transfers between devices with their start and end apart: 4, of which 3 were waited for; matrix products, arithmetic and copies ran while one was open for 1% of the time, Pallas kernels for 0%

commit v1 on v0

v1 whole, which is shorter than its diff:
```python
import functools

import jax
import jax.numpy as jnp
from jax import lax
from jax.experimental import pallas as pl
from jax.experimental.pallas import tpu as pltpu
from jax.sharding import PartitionSpec as P

HIGH = lax.Precision.HIGHEST
MESH = pl.DeviceIdType.MESH
F32 = jnp.float32
BLK = 128
WIDE = 2 * BLK
OUTER = 32
CHUNK = 256
CORRECT = 1


def dot(a, b, ca, cb):
    dims = (((ca,), (cb,)), ((), ()))
    return lax.dot_general(a, b, dims, precision=HIGH, preferred_element_type=F32)


def bdot(a, b, ca, cb):
    dims = (((ca,), (cb,)), ((), ()))
    return lax.dot_general(a, b, dims, preferred_element_type=F32)


def halves(a):
    high = a.astype(jnp.bfloat16)
    return high, (a - high.astype(F32)).astype(jnp.bfloat16)


def dot3(a, b, ca, cb):
    ah, al = halves(a)
    bh, bl = halves(b)
    return bdot(al, bh, ca, cb) + bdot(ah, bl, ca, cb) + bdot(ah, bh, ca, cb)


def wide(v):
    return jnp.concatenate([v] * (WIDE // 128), axis=1)


def panel(s, splat, k, end):
    c0 = (k // 128) * 128
    own = s[pl.ds(k, 8), pl.ds(c0, 128)]
    for j in range(8):
        at = k - c0 + j
        splat[j] = jnp.broadcast_to(own[:, at : at + 1], (8, 128))
    e = {(i, j): splat[j, i : i + 1, :] for j in range(8) for i in range(j, 8)}
    lanes = lax.broadcasted_iota(jnp.int32, (1, WIDE), 1)
    rows = []
    for i in range(8):
        row = s[pl.ds(k + i, 1), :]
        row = jnp.where((lanes >= k) & (lanes < k + 8), 0.0, row)
        rows.append(jnp.where(lanes == k + i, 1.0, row))
    l = {}
    scale = []
    for a in range(0, 8, 2):
        b = a + 1
        p, q, t = e[a, a], e[b, a], e[b, b]
        ra, rd = lax.rsqrt(p), lax.rsqrt(p * t - q * q)
        rb = rd * (p * ra)
        scale += [ra, rb]
        l[b, a] = q * ra
        for i in range(b + 1, 8):
            l[i, a] = e[i, a] * ra
            l[i, b] = (e[i, b] - l[i, a] * l[b, a]) * rb
        for j in range(b + 1, 8):
            for i in range(j, 8):
                e[i, j] = e[i, j] - (l[i, a] * l[j, a] + l[i, b] * l[j, b])
        rows[a] = rows[a] * wide(ra)
        rows[b] = (rows[b] - wide(l[b, a]) * rows[a]) * wide(rb)
        for i in range(b + 1, 8):
            rows[i] = rows[i] - (wide(l[i, a]) * rows[a] + wide(l[i, b]) * rows[b])
    for i in range(8):
        s[pl.ds(k + i, 1), :] = rows[i]
    full = [jnp.broadcast_to(row, (8, WIDE)) for row in rows]
    lanes = lax.broadcasted_iota(jnp.int32, (8, WIDE), 1)
    inside = (lanes >= k) & (lanes < k + 8)
    for g in range(k + 8, end, 8):
        old = s[pl.ds(g, 8), :]
        m = []
        for j in range(8):
            at = k + j
            t = jnp.broadcast_to(old[:, at : at + 1], (8, 128))
            for jj in range(j):
                t = t - m[jj] * jnp.broadcast_to(l[j, jj], (8, 128))
            m.append(t * jnp.broadcast_to(scale[j], (8, 128)))
        new = jnp.where(inside, 0.0, old)
        for j in range(8):
            new = new - wide(m[j]) * full[j]
        s[pl.ds(g, 8), :] = new


def factor_inverse(s, splat):
    for b0 in range(0, WIDE, OUTER):
        b1 = b0 + OUTER
        for k in range(b0, b1, 8):
            panel(s, splat, k, b1)
        if b1 == WIDE:
            break
        lanes = lax.broadcasted_iota(jnp.int32, (OUTER, WIDE), 1)
        row = lax.broadcasted_iota(jnp.int32, (OUTER, WIDE), 0)
        block = jnp.where((lanes < b1) & (lanes > row + b0), 0.0, s[pl.ds(b0, OUTER), :])
        rest = s[pl.ds(b1, WIDE - b1), :]
        c0 = (b0 // 128) * 128
        near = lax.broadcasted_iota(jnp.int32, (1, 128), 1) + c0
        inverse = jnp.where((near >= b0) & (near < b1), block[:, c0 : c0 + 128], 0.0)
        factor = dot3(rest[:, c0 : c0 + 128], inverse, 1, 1)
        lanes = lax.broadcasted_iota(jnp.int32, (1, WIDE), 1)
        rest = jnp.where((lanes >= b0) & (lanes < b1), 0.0, rest)
        s[pl.ds(b1, WIDE - b1), :] = rest - dot3(factor, block, 1, 0)


def rotation(gram, s, splat):
    square = dot(gram, gram, 1, 0)
    s[...] = dot(square, square, 1, 0)
    factor_inverse(s, splat)
    row = lax.broadcasted_iota(jnp.int32, (WIDE, WIDE), 0)
    col = lax.broadcasted_iota(jnp.int32, (WIDE, WIDE), 1)
    turn = dot(square, jnp.where(row >= col, s[...], 0.0), 1, 1)
    for _ in range(CORRECT):
        over = dot(turn, turn, 0, 0)
        over = jnp.where(row == col, (over - 1.0) * 0.5, jnp.where(row < col, over, 0.0))
        turn = turn - dot(turn, over, 1, 0)
    return turn


def kernel(
    pairs, gram_scale, mass_scale,
    a_ref, v_ref, ao_ref, vo_ref, m_ref,
    sent, got, done, s, splat, hh, hl, qh, ql,
    part, near, half, far, full, mine, groups,
    up_s, up_r, dn_s, dn_r, sum_s, sum_r, grp_s, grp_r, out_sem,
):
    rows_a, rows_v = a_ref.shape[0], v_ref.shape[0]
    chunks_a, chunks = rows_a // CHUNK, (rows_a + rows_v) // CHUNK
    inner = min(8, pairs)
    outer = pairs // inner
    p, r = lax.axis_index("pair"), lax.axis_index("row")
    core = lax.rem(r, 2)
    beside = r + 1 - 2 * core
    across = lax.rem(r + 2, 4)
    pa, pb = p // inner, lax.rem(p, inner)
    up_from = (pairs - p) // pairs
    has_up, has_dn = p < pairs - 1, p > 0

    def group_device(stage, other):
        return (pa * inner + other, r) if stage == 0 else (other * inner + pb, r)

    sizes, place = (inner, outer), (pb, pa)

    bar = pltpu.get_barrier_semaphore()

    def hello(device):
        pl.semaphore_signal(bar, 1, device_id=device, device_id_type=MESH)

    hello((p, beside))
    hello((p, across))
    for stage in range(2):
        for k in range(1, sizes[stage]):
            hello(group_device(stage, lax.rem(place[stage] + k, sizes[stage])))

    @pl.when(has_up)
    def _():
        hello((p + 1, r))

    @pl.when(has_dn)
    def _():
        hello((p - 1, r))

    def add_gram(x):
        high, low = halves(x)
        hh[...] += bdot(high, high, 0, 0)
        hl[...] += bdot(high, low, 0, 0)

    def clear_gram():
        hh[...] = jnp.zeros_like(hh)
        hl[...] = jnp.zeros_like(hl)

    def sum_over_row(rnd):
        cross = hl[...]
        gram = hh[...] + (cross + cross.T)
        part[rnd, 0, pl.ds(0, 128), :] = gram[:128, :128]
        part[rnd, 0, pl.ds(128, 64), :] = gram[:64, 128:]
        part[rnd, 1, pl.ds(0, 64), :] = gram[64:128, 128:]
        part[rnd, 1, pl.ds(64, 128), :] = gram[128:, 128:]

        def move(step, src, dst, device):
            copy = pltpu.make_async_remote_copy(
                src_ref=src, dst_ref=dst, send_sem=sum_s.at[rnd, step], recv_sem=sum_r.at[rnd, step],
                device_id=device, device_id_type=MESH,
            )
            copy.start()
            copy.wait()

        if rnd == 0:
            ends = up_from + (p + 1) // pairs
            pl.semaphore_wait(bar, 2 + inner - 1 + outer - 1 + 2 - ends)

        move(0, part.at[rnd, 1 - core], near.at[rnd], (p, beside))
        half[rnd] = part[rnd, core] + near[rnd]
        move(1, half.at[rnd], far.at[rnd], (p, across))
        full[rnd, core] = half[rnd] + far[rnd]
        move(2, full.at[rnd, core], full.at[rnd, core], (p, beside))
        top = full[rnd, 0, pl.ds(0, 128), :]
        mid = jnp.concatenate([full[rnd, 0, pl.ds(128, 64), :], full[rnd, 1, pl.ds(0, 64), :]], axis=0)
        low = full[rnd, 1, pl.ds(64, 128), :]
        return jnp.concatenate(
            [jnp.concatenate([top, mid], axis=1), jnp.concatenate([mid.T, low], axis=1)], axis=0
        )

    def off_mass(gram):
        row = lax.broadcasted_iota(jnp.int32, (WIDE, WIDE), 0)
        col = lax.broadcasted_iota(jnp.int32, (WIDE, WIDE), 1)
        squares = jnp.where(row == col, 0.0, gram * gram)
        return jnp.sum(jnp.sum(squares, axis=1, keepdims=True), axis=0, keepdims=True)

    def take_turn(gram):
        high, low = halves(rotation(gram * gram_scale, s, splat))
        qh[...] = high
        ql[...] = low

    def turned(x):
        high, low = halves(x)
        return bdot(low, qh[...], 1, 0) + bdot(high, ql[...], 1, 0) + bdot(high, qh[...], 1, 0)

    def at(c):
        return pl.ds(pl.multiple_of(c * CHUNK, CHUNK), CHUNK)

    def up(c):
        return pltpu.make_async_remote_copy(
            src_ref=sent.at[up_from, at(c)], dst_ref=got.at[0, at(c)], send_sem=up_s.at[c], recv_sem=up_r.at[c],
            device_id=(p + 1, r), device_id_type=MESH,
        )

    def down(c):
        return pltpu.make_async_remote_copy(
            src_ref=sent.at[1, at(c)], dst_ref=got.at[1, at(c)], send_sem=dn_s.at[c], recv_sem=dn_r.at[c],
            device_id=(p - 1, r), device_id_type=MESH,
        )

    def send(c):
        @pl.when(has_up)
        def _():
            up(c).start()

        @pl.when(has_dn)
        def _():
            down(c).start()

    def receive(c):
        @pl.when(has_dn)
        def _():
            up(c).wait_recv()

        @pl.when(has_up)
        def _():
            down(c).wait_recv()

    def turn_chunk(c, x):
        y = turned(x)
        sent[0, at(c), :] = y[:, :BLK]
        sent[1, at(c), :] = y[:, BLK:]

        @pl.when(p == 0)
        def _():
            got[0, at(c), :] = y[:, :BLK]

        @pl.when(p == pairs - 1)
        def _():
            got[1, at(c), :] = y[:, :BLK]

    def arrived(c):
        return jnp.concatenate([got[0, at(c), :], got[1, at(c), :]], axis=1)

    def group_copy(stage, k):
        here = place[stage]
        other = lax.rem(here + k, sizes[stage])
        return pltpu.make_async_remote_copy(
            src_ref=mine.at[stage], dst_ref=groups.at[stage, here], send_sem=grp_s.at[stage, k],
            recv_sem=grp_r.at[stage, here], device_id=group_device(stage, other), device_id_type=MESH,
        )

    def group_send(stage, value):
        mine[stage] = value
        groups[stage, place[stage]] = value
        for k in range(1, sizes[stage]):
            group_copy(stage, k).start()

    def group_sum(stage):
        for k in range(1, sizes[stage]):
            other = lax.rem(place[stage] + k, sizes[stage])
            pltpu.make_async_remote_copy(
                src_ref=mine.at[stage], dst_ref=groups.at[stage, other], send_sem=grp_s.at[stage, k],
                recv_sem=grp_r.at[stage, other], device_id=group_device(stage, other), device_id_type=MESH,
            ).wait_recv()
        total = groups[stage, 0]
        for other in range(1, sizes[stage]):
            total = total + groups[stage, other]
        return total

    clear_gram()

    @pl.loop(0, chunks_a)
    def _(c):
        add_gram(a_ref[at(c), :])

    gram = sum_over_row(0)
    mass_one = off_mass(gram)
    take_turn(gram)

    @pl.loop(0, chunks_a)
    def _(c):
        turn_chunk(c, a_ref[at(c), :])
        send(c)

    @pl.loop(chunks_a, chunks)
    def _(c):
        turn_chunk(c, v_ref[at(c - chunks_a), :])

    clear_gram()
    late = chunks_a - (chunks - chunks_a)

    @pl.loop(0, late)
    def _(c):
        receive(c)
        add_gram(arrived(c))

    @pl.loop(late, chunks_a)
    def _(c):
        receive(c)
        send(c + chunks - chunks_a)
        add_gram(arrived(c))

    gram = sum_over_row(1)
    mass_two = off_mass(gram)
    first = lax.broadcasted_iota(jnp.int32, (8, 128), 1) == 0
    both = jnp.where(first, jnp.broadcast_to(mass_one, (8, 128)), jnp.broadcast_to(mass_two, (8, 128)))
    group_send(0, both)
    take_turn(gram)
    group_send(1, group_sum(0))

    def out(c):
        ref, c0 = (ao_ref, c) if c < chunks_a else (vo_ref, c - chunks_a)
        return pltpu.make_async_copy(done.at[at(c)], ref.at[pl.ds(c0 * CHUNK, CHUNK)], out_sem.at[c])

    for c in range(chunks):
        if c >= chunks_a:
            receive(c)
        done[at(c), :] = turned(arrived(c))
        out(c).start()
    m_ref[...] = group_sum(1) * mass_scale

    @pl.loop(0, chunks)
    def _(c):
        @pl.when(has_up)
        def _():
            up(c).wait_send()

        @pl.when(has_dn)
        def _():
            down(c).wait_send()

    for stage in range(2):
        for k in range(1, sizes[stage]):
            group_copy(stage, k).wait_send()
    for c in range(chunks):
        out(c).wait()


def local(pairs, matrix, vectors):
    rows_a, rows_v = matrix.shape[0], vectors.shape[0]
    total_rows = float(rows_a * lax.axis_size("row"))
    chunks = (rows_a + rows_v) // CHUNK
    inner = min(8, pairs)
    body = functools.partial(kernel, pairs, 2.0**-13, 1.0 / (total_rows * total_rows * float(pairs)))
    dma = pltpu.SemaphoreType.DMA
    vmem = pltpu.VMEM
    matrix_out, vectors_out, mass = pl.pallas_call(
        body,
        out_shape=(
            jax.ShapeDtypeStruct(matrix.shape, F32),
            jax.ShapeDtypeStruct(vectors.shape, F32),
            jax.ShapeDtypeStruct((8, 128), F32),
        ),
        in_specs=[pl.BlockSpec(memory_space=vmem)] * 2,
        out_specs=(
            pl.BlockSpec(memory_space=pl.ANY),
            pl.BlockSpec(memory_space=pl.ANY),
            pl.BlockSpec(memory_space=vmem),
        ),
        scratch_shapes=[
            vmem((2, rows_a + rows_v, BLK), F32),
            vmem((2, rows_a + rows_v, BLK), F32),
            vmem((rows_a + rows_v, WIDE), F32),
            vmem((WIDE, WIDE), F32),
            vmem((8, 8, 128), F32),
            vmem((WIDE, WIDE), F32),
            vmem((WIDE, WIDE), F32),
            vmem((WIDE, WIDE), jnp.bfloat16),
            vmem((WIDE, WIDE), jnp.bfloat16),
            vmem((2, 2, 192, 128), F32),
            vmem((2, 192, 128), F32),
            vmem((2, 192, 128), F32),
            vmem((2, 192, 128), F32),
            vmem((2, 2, 192, 128), F32),
            vmem((2, 8, 128), F32),
            vmem((2, 8, 8, 128), F32),
            dma((chunks,)),
            dma((chunks,)),
            dma((chunks,)),
            dma((chunks,)),
            dma((2, 3)),
            dma((2, 3)),
            dma((2, 8)),
            dma((2, 8)),
            dma((chunks,)),
        ],
        compiler_params=pltpu.CompilerParams(
            collective_id=0, has_side_effects=True, vmem_limit_bytes=40 * 2**20
        ),
    )(matrix, vectors)
    return matrix_out, vectors_out, mass[0, :2]


def solution(mesh):
    return jax.shard_map(
        functools.partial(local, mesh.shape["pair"]),
        mesh=mesh,
        in_specs=(P("row", "pair"), P("row", "pair")),
        out_specs=(P("row", "pair"), P("row", "pair"), P()),
        check_vma=False,
    )
```

time: 642 us -> 123 us (0.19)
  the two profiles are of different devices: /device:TPU:2 before, /device:TPU:1 now
where the time goes in v1:
time: 123 us
  Pallas kernels  117 us (95%)
  local copies, waits for them, and re-layouts  5.61 us (5%)
    pallas_call x1, Pallas kernels, local(): pl.pallas_call(body, out_shape=(jax.ShapeDtypeStruct(matrix.shape, F32),...  117 us
    unnamed x6, local copies, waits for them, and re-layouts  5.1 us

profile of v1, /device:TPU:1, one launch (start us, length us, event | category | flops | bytes accessed | tf_op | source)
XLA Modules:
  0.0 123.2 jit_solution(5884460854107305644)
XLA Ops:
  0.6 0.0 copy-start
  0.6 1.6 %copy-done = f32[2048,256]{1,0:T(8,128)S(1)} copy-done((f32[2048,256]{1,0:T(8,128)S(1)}, f32[2048,256]{1,0:T(8,128)}, u32[]{:S(2)}) %copy-start) | copy-done | bytes 2097176
  2.2 0.0 copy-start.1
  2.2 1.2 copy-done.1
  3.4 117.0 %shard_map.49 = (f32[2048,256]{1,0:T(8,128)S(1)}, f32[1024,256]{1,0:T(8,128)S(1)}, f32[8,128]{1,0:T(8,128)S(1)}) custom-call(f32[2048,256]{1,0:T(8,128)S(1)} %copy-done, f32[1024,256]{1,0:T(8,128)S(1)} %copy-done.1), custom_call_target="tpu_custom_call" | custom-call | tf_op jit(solution)/shard_map/pallas_call | solution.py:382
  120.4 0.5 slice_bitcast_fusion
  120.9 1.3 %copy.7 = f32[2048,256]{1,0:T(8,128)} copy(f32[2048,256]{1,0:T(8,128)S(1)} %get-tuple-element.12) | data formatting | bytes 4194304
  122.2 1.0 copy.8
Async XLA Ops:
  0.6 1.6 %copy-start = (f32[2048,256]{1,0:T(8,128)S(1)}, f32[2048,256]{1,0:T(8,128)}, u32[]{:S(2)}) copy-start(f32[2048,256]{1,0:T(8,128)} %a_ref.1) | copy-start | bytes 6291460
  2.2 1.2 copy-start.1

commit v2 on v1

--- a/solution.py
+++ b/solution.py
@@ -13,7 +13,13 @@
 BLK = 128
 WIDE = 2 * BLK
 OUTER = 32
+PIECE = 512
 CHUNK = 256
+SMALL = 128
+RAW = 3
+RAW_FIRST = 128
+EARLY = 1
+MIDDLE = 1
 CORRECT = 1
 
 
@@ -131,26 +137,37 @@
 def kernel(
     pairs, gram_scale, mass_scale,
     a_ref, v_ref, ao_ref, vo_ref, m_ref,
-    sent, got, done, s, splat, hh, hl, qh, ql,
+    held, sent, got, done, raw, relayed, s, splat, hh, hl, qh, ql, ph, pl_, q_out, q_in,
     part, near, half, far, full, mine, groups,
-    up_s, up_r, dn_s, dn_r, sum_s, sum_r, grp_s, grp_r, out_sem,
+    in_sem, up_s, up_r, dn_s, dn_r, raw_s, raw_r, rel_s, rel_r, turn_s, turn_r, sum_s, sum_r, grp_s, grp_r, out_sem,
 ):
     rows_a, rows_v = a_ref.shape[0], v_ref.shape[0]
-    chunks_a, chunks = rows_a // CHUNK, (rows_a + rows_v) // CHUNK
+    chunks_a, small = rows_a // CHUNK, rows_v // SMALL
     inner = min(8, pairs)
     outer = pairs // inner
     p, r = lax.axis_index("pair"), lax.axis_index("row")
     core = lax.rem(r, 2)
     beside = r + 1 - 2 * core
     across = lax.rem(r + 2, 4)
+    odd = lax.rem(p, 2)
+    mate = p + 1 - 2 * odd
+    to = p + 2 - 4 * odd
+    source = p - 2 + 4 * odd
     pa, pb = p // inner, lax.rem(p, inner)
     up_from = (pairs - p) // pairs
     has_up, has_dn = p < pairs - 1, p > 0
+    has_to = (to >= 0) & (to < pairs)
+    has_source = (source >= 0) & (source < pairs)
 
     def group_device(stage, other):
         return (pa * inner + other, r) if stage == 0 else (other * inner + pb, r)
 
     sizes, place = (inner, outer), (pb, pa)
+
+    def remote(src, dst, send_sem, recv_sem, device):
+        return pltpu.make_async_remote_copy(
+            src_ref=src, dst_ref=dst, send_sem=send_sem, recv_sem=recv_sem, device_id=device, device_id_type=MESH
+        )
 
     bar = pltpu.get_barrier_semaphore()
 
@@ -163,13 +180,29 @@
         for k in range(1, sizes[stage]):
             hello(group_device(stage, lax.rem(place[stage] + k, sizes[stage])))
 
-    @pl.when(has_up)
-    def _():
-        hello((p + 1, r))
-
-    @pl.when(has_dn)
-    def _():
-        hello((p - 1, r))
+    for there, device in ((has_up, p + 1), (has_dn, p - 1), (has_to, to), (has_source, source)):
+
+        @pl.when(there)
+        def _(device=device):
+            hello((device, r))
+
+    def barrier():
+        ends = up_from + (p + 1) // pairs
+        ends = ends + (pairs + 1 - p) // pairs + (p + 2) // pairs
+        pl.semaphore_wait(bar, 2 + inner - 1 + outer - 1 + 4 - ends)
+
+    def rows(c, size=CHUNK):
+        return pl.ds(pl.multiple_of(c * size, size), size)
+
+    pieces = rows_a // PIECE
+
+    def load(i):
+        src = a_ref.at[rows(i, PIECE)] if i < pieces else v_ref
+        size = PIECE if i < pieces else rows_v
+        return pltpu.make_async_copy(src, held.at[pl.ds(i * PIECE, size)], in_sem.at[i])
+
+    for i in range(pieces + 1):
+        load(i).start()
 
     def add_gram(x):
         high, low = halves(x)
@@ -180,7 +213,7 @@
         hh[...] = jnp.zeros_like(hh)
         hl[...] = jnp.zeros_like(hl)
 
-    def sum_over_row(rnd):
+    def sum_over_row(rnd, between):
         cross = hl[...]
         gram = hh[...] + (cross + cross.T)
         part[rnd, 0, pl.ds(0, 128), :] = gram[:128, :128]
@@ -189,22 +222,20 @@
         part[rnd, 1, pl.ds(64, 128), :] = gram[128:, 128:]
 
         def move(step, src, dst, device):
-            copy = pltpu.make_async_remote_copy(
-                src_ref=src, dst_ref=dst, send_sem=sum_s.at[rnd, step], recv_sem=sum_r.at[rnd, step],
-                device_id=device, device_id_type=MESH,
-            )
-            copy.start()
-            copy.wait()
-
-        if rnd == 0:
-            ends = up_from + (p + 1) // pairs
-            pl.semaphore_wait(bar, 2 + inner - 1 + outer - 1 + 2 - ends)
-
-        move(0, part.at[rnd, 1 - core], near.at[rnd], (p, beside))
+            return remote(src, dst, sum_s.at[rnd, step], sum_r.at[rnd, step], device)
+
+        copy = move(0, part.at[rnd, 1 - core], near.at[rnd], (p, beside))
+        copy.start()
+        copy.wait()
         half[rnd] = part[rnd, core] + near[rnd]
-        move(1, half.at[rnd], far.at[rnd], (p, across))
+        copy = move(1, half.at[rnd], far.at[rnd], (p, across))
+        copy.start()
+        between()
+        copy.wait()
         full[rnd, core] = half[rnd] + far[rnd]
-        move(2, full.at[rnd, core], full.at[rnd, core], (p, beside))
+        copy = move(2, full.at[rnd, core], full.at[rnd, core], (p, beside))
+        copy.start()
+        copy.wait()
         top = full[rnd, 0, pl.ds(0, 128), :]
         mid = jnp.concatenate([full[rnd, 0, pl.ds(128, 64), :], full[rnd, 1, pl.ds(0, 64), :]], axis=0)
         low = full[rnd, 1, pl.ds(64, 128), :]
@@ -219,28 +250,41 @@
         return jnp.sum(jnp.sum(squares, axis=1, keepdims=True), axis=0, keepdims=True)
 
     def take_turn(gram):
-        high, low = halves(rotation(gram * gram_scale, s, splat))
+        turn = rotation(gram * gram_scale, s, splat)
+        high, low = halves(turn)
         qh[...] = high
         ql[...] = low
-
-    def turned(x):
+        return turn
+
+    def turned(x, qh=qh, ql=ql):
         high, low = halves(x)
         return bdot(low, qh[...], 1, 0) + bdot(high, ql[...], 1, 0) + bdot(high, qh[...], 1, 0)
 
-    def at(c):
-        return pl.ds(pl.multiple_of(c * CHUNK, CHUNK), CHUNK)
+    def chunk(c):
+        return c, rows(c)
+
+    def small_chunk(v):
+        return chunks_a + v, pl.ds(pl.multiple_of(rows_a + v * SMALL, SMALL), SMALL)
 
     def up(c):
-        return pltpu.make_async_remote_copy(
-            src_ref=sent.at[up_from, at(c)], dst_ref=got.at[0, at(c)], send_sem=up_s.at[c], recv_sem=up_r.at[c],
-            device_id=(p + 1, r), device_id_type=MESH,
-        )
+        src, dst = sent.at[up_from, c[1]], got.at[0, c[1]]
+        return remote(src, dst, up_s.at[c[0]], up_r.at[c[0]], (p + 1, r))
 
     def down(c):
-        return pltpu.make_async_remote_copy(
-            src_ref=sent.at[1, at(c)], dst_ref=got.at[1, at(c)], send_sem=dn_s.at[c], recv_sem=dn_r.at[c],
-            device_id=(p - 1, r), device_id_type=MESH,
-        )
+        src, dst = sent.at[1, c[1]], got.at[1, c[1]]
+        return remote(src, dst, dn_s.at[c[0]], dn_r.at[c[0]], (p - 1, r))
+
+    def raw_copy(i):
+        at = pl.ds(0, RAW_FIRST) if i == 0 else pl.ds(RAW_FIRST, RAW * CHUNK - RAW_FIRST)
+        return remote(a_ref.at[at], raw.at[at], raw_s.at[i], raw_r.at[i], (mate, r))
+
+    def relay(c):
+        return remote(relayed.at[rows(c)], got.at[odd, rows(c)], rel_s.at[c], rel_r.at[c], (to, r))
+
+    def turn_copy(step):
+        if step == 0:
+            return remote(q_out.at[core], q_in.at[core], turn_s.at[0], turn_r.at[0], (mate, r))
+        return remote(q_in.at[core], q_in.at[core], turn_s.at[1], turn_r.at[1], (p, beside))
 
     def send(c):
         @pl.when(has_up)
@@ -260,29 +304,29 @@
         def _():
             down(c).wait_recv()
 
-    def turn_chunk(c, x):
-        y = turned(x)
-        sent[0, at(c), :] = y[:, :BLK]
-        sent[1, at(c), :] = y[:, BLK:]
-
+    def keep_ends(at, y):
         @pl.when(p == 0)
         def _():
-            got[0, at(c), :] = y[:, :BLK]
+            got[0, at, :] = y[:, :BLK]
 
         @pl.when(p == pairs - 1)
         def _():
-            got[1, at(c), :] = y[:, :BLK]
-
-    def arrived(c):
-        return jnp.concatenate([got[0, at(c), :], got[1, at(c), :]], axis=1)
+            got[1, at, :] = y[:, :BLK]
+
+    def turn_rows(at):
+        y = turned(held[at, :])
+        sent[0, at, :] = y[:, :BLK]
+        sent[1, at, :] = y[:, BLK:]
+        keep_ends(at, y)
+
+    def arrived(at):
+        return jnp.concatenate([got[0, at, :], got[1, at, :]], axis=1)
 
     def group_copy(stage, k):
         here = place[stage]
         other = lax.rem(here + k, sizes[stage])
-        return pltpu.make_async_remote_copy(
-            src_ref=mine.at[stage], dst_ref=groups.at[stage, here], send_sem=grp_s.at[stage, k],
-            recv_sem=grp_r.at[stage, here], device_id=group_device(stage, other), device_id_type=MESH,
-        )
+        dst = groups.at[stage, here]
+        return remote(mine.at[stage], dst, grp_s.at[stage, k], grp_r.at[stage, here], group_device(stage, other))
 
     def group_send(stage, value):
         mine[stage] = value
@@ -293,9 +337,9 @@
     def group_sum(stage):
         for k in range(1, sizes[stage]):
             other = lax.rem(place[stage] + k, sizes[stage])
-            pltpu.make_async_remote_copy(
-                src_ref=mine.at[stage], dst_ref=groups.at[stage, other], send_sem=grp_s.at[stage, k],
-                recv_sem=grp_r.at[stage, other], device_id=group_device(stage, other), device_id_type=MESH,
+            dst = groups.at[stage, other]
+            remote(
+                mine.at[stage], dst, grp_s.at[stage, k], grp_r.at[stage, other], group_device(stage, other)
             ).wait_recv()
         total = groups[stage, 0]
         for other in range(1, sizes[stage]):
@@ -303,59 +347,118 @@
         return total
 
     clear_gram()
-
-    @pl.loop(0, chunks_a)
-    def _(c):
-        add_gram(a_ref[at(c), :])
-
-    gram = sum_over_row(0)
+    for i in range(pieces):
+        load(i).wait()
+        if i == pieces // 2:
+            barrier()
+            raw_copy(0).start()
+        add_gram(held[rows(i, PIECE), :])
+
+    def rest_of_raw():
+        raw_copy(1).start()
+
+    gram = sum_over_row(0, rest_of_raw)
     mass_one = off_mass(gram)
-    take_turn(gram)
-
-    @pl.loop(0, chunks_a)
-    def _(c):
-        turn_chunk(c, a_ref[at(c), :])
-        send(c)
-
-    @pl.loop(chunks_a, chunks)
-    def _(c):
-        turn_chunk(c, v_ref[at(c - chunks_a), :])
+    turn = take_turn(gram)
+    q_out[0] = turn[:BLK]
+    q_out[1] = turn[BLK:]
+    turn_copy(0).start()
+
+    @pl.loop(RAW, chunks_a)
+    def _(c):
+        turn_rows(rows(c))
+        send(chunk(c))
+
+    turn_copy(0).wait_recv()
+    turn_copy(1).start()
+    turn_copy(1).wait()
+    for i in range(2):
+        high, low = halves(q_in[i])
+        ph[pl.ds(i * BLK, BLK), :] = high
+        pl_[pl.ds(i * BLK, BLK), :] = low
+
+    raw_copy(0).wait_recv()
+    raw_copy(1).wait_recv()
+
+    @pl.loop(0, RAW)
+    def _(c):
+        y = turned(raw[rows(c), :], ph, pl_)
+        top, bottom = y[:, :BLK], y[:, BLK:]
+        got[1 - odd, rows(c), :] = jnp.where((odd == 0) | (p == 1), bottom, top)
+        relayed[rows(c), :] = jnp.where(odd == 0, top, bottom)
+
+        @pl.when(has_to)
+        def _():
+            relay(c).start()
+
+        @pl.when((p == 0) | (p == pairs - 1))
+        def _():
+            keep_ends(rows(c), turned(held[rows(c), :]))
+
+    load(pieces).wait()
+
+    @pl.loop(0, rows_v // PIECE)
+    def _(c):
+        turn_rows(pl.ds(pl.multiple_of(rows_a + c * PIECE, PIECE), PIECE))
+
+    for v in range(EARLY):
+        send(small_chunk(v))
 
     clear_gram()
-    late = chunks_a - (chunks - chunks_a)
-
-    @pl.loop(0, late)
-    def _(c):
-        receive(c)
-        add_gram(arrived(c))
-
-    @pl.loop(late, chunks_a)
-    def _(c):
-        receive(c)
-        send(c + chunks - chunks_a)
-        add_gram(arrived(c))
-
-    gram = sum_over_row(1)
+
+    @pl.loop(0, RAW)
+    def _(c):
+        @pl.when(has_source)
+        def _():
+            relay(c).wait_recv()
+
+        add_gram(arrived(rows(c)))
+
+    @pl.loop(RAW, chunks_a)
+    def _(c):
+        receive(chunk(c))
+        add_gram(arrived(rows(c)))
+
+    def some_vectors():
+        for v in range(EARLY, EARLY + MIDDLE):
+            send(small_chunk(v))
+
+    gram = sum_over_row(1, some_vectors)
     mass_two = off_mass(gram)
     first = lax.broadcasted_iota(jnp.int32, (8, 128), 1) == 0
     both = jnp.where(first, jnp.broadcast_to(mass_one, (8, 128)), jnp.broadcast_to(mass_two, (8, 128)))
     group_send(0, both)
+
+    @pl.loop(EARLY + MIDDLE, small)
+    def _(v):
+        send(small_chunk(v))
+
     take_turn(gram)
     group_send(1, group_sum(0))
 
+    pieces_v = rows_v // SMALL
+
     def out(c):
-        ref, c0 = (ao_ref, c) if c < chunks_a else (vo_ref, c - chunks_a)
-        return pltpu.make_async_copy(done.at[at(c)], ref.at[pl.ds(c0 * CHUNK, CHUNK)], out_sem.at[c])
-
-    for c in range(chunks):
-        if c >= chunks_a:
-            receive(c)
-        done[at(c), :] = turned(arrived(c))
+        return pltpu.make_async_copy(done.at[rows(c, PIECE)], ao_ref.at[rows(c, PIECE)], out_sem.at[c])
+
+    def out_v(v):
+        return pltpu.make_async_copy(done.at[small_chunk(v)[1]], vo_ref.at[rows(v, SMALL)], out_sem.at[pieces + v])
+
+    @pl.loop(0, pieces)
+    def _(c):
+        done[rows(c, PIECE), :] = turned(arrived(rows(c, PIECE)))
         out(c).start()
+
+    @pl.loop(0, pieces_v)
+    def _(v):
+        receive(small_chunk(v))
+        at = small_chunk(v)[1]
+        done[at, :] = turned(arrived(at))
+        out_v(v).start()
+
     m_ref[...] = group_sum(1) * mass_scale
 
-    @pl.loop(0, chunks)
-    def _(c):
+    def sent_all(c):
         @pl.when(has_up)
         def _():
             up(c).wait_send()
@@ -364,18 +467,41 @@
         def _():
             down(c).wait_send()
 
+    @pl.loop(RAW, chunks_a)
+    def _(c):
+        sent_all(chunk(c))
+
+    @pl.loop(0, small)
+    def _(v):
+        sent_all(small_chunk(v))
+
+    raw_copy(0).wait_send()
+    raw_copy(1).wait_send()
+
+    @pl.loop(0, RAW)
+    def _(c):
+        @pl.when(has_to)
+        def _():
+            relay(c).wait_send()
+
+    turn_copy(0).wait_send()
     for stage in range(2):
         for k in range(1, sizes[stage]):
             group_copy(stage, k).wait_send()
-    for c in range(chunks):
+
+    @pl.loop(0, pieces)
+    def _(c):
         out(c).wait()
+
+    @pl.loop(0, pieces_v)
+    def _(v):
+        out_v(v).wait()
 
 
 def local(pairs, matrix, vectors):
     rows_a, rows_v = matrix.shape[0], vectors.shape[0]
     total_rows = float(rows_a * lax.axis_size("row"))
-    chunks = (rows_a + rows_v) // CHUNK
-    inner = min(8, pairs)
+    sends = rows_a // CHUNK + rows_v // SMALL
     body = functools.partial(kernel, pairs, 2.0**-13, 1.0 / (total_rows * total_rows * float(pairs)))
     dma = pltpu.SemaphoreType.DMA
     vmem = pltpu.VMEM
@@ -386,22 +512,29 @@
             jax.ShapeDtypeStruct(vectors.shape, F32),
             jax.ShapeDtypeStruct((8, 128), F32),
         ),
-        in_specs=[pl.BlockSpec(memory_space=vmem)] * 2,
+        in_specs=[pl.BlockSpec(memory_space=pltpu.HBM)] * 2,
         out_specs=(
             pl.BlockSpec(memory_space=pl.ANY),
             pl.BlockSpec(memory_space=pl.ANY),
             pl.BlockSpec(memory_space=vmem),
         ),
         scratch_shapes=[
+            vmem((rows_a + rows_v, WIDE), F32),
             vmem((2, rows_a + rows_v, BLK), F32),
             vmem((2, rows_a + rows_v, BLK), F32),
             vmem((rows_a + rows_v, WIDE), F32),
+            vmem((RAW * CHUNK, WIDE), F32),
+            vmem((RAW * CHUNK, BLK), F32),
             vmem((WIDE, WIDE), F32),
             vmem((8, 8, 128), F32),
             vmem((WIDE, WIDE), F32),
             vmem((WIDE, WIDE), F32),
             vmem((WIDE, WIDE), jnp.bfloat16),
             vmem((WIDE, WIDE), jnp.bfloat16),
+            vmem((WIDE, WIDE), jnp.bfloat16),
+            vmem((WIDE, WIDE), jnp.bfloat16),
+            vmem((2, BLK, WIDE), F32),
+            vmem((2, BLK, WIDE), F32),
             vmem((2, 2, 192, 128), F32),
             vmem((2, 192, 128), F32),
             vmem((2, 192, 128), F32),
@@ -409,15 +542,22 @@
             vmem((2, 2, 192, 128), F32),
             vmem((2, 8, 128), F32),
             vmem((2, 8, 8, 128), F32),
-            dma((chunks,)),
-            dma((chunks,)),
-            dma((chunks,)),
-            dma((chunks,)),
+            dma((rows_a // PIECE + 1,)),
+            dma((sends,)),
+            dma((sends,)),
+            dma((sends,)),
+            dma((sends,)),
+            dma((2,)),
+            dma((2,)),
+            dma((RAW,)),
+            dma((RAW,)),
+            dma((2,)),
+            dma((2,)),
             dma((2, 3)),
             dma((2, 3)),
             dma((2, 8)),
             dma((2, 8)),
-            dma((chunks,)),
+            dma((rows_a // PIECE + rows_v // SMALL,)),
         ],
         compiler_params=pltpu.CompilerParams(
             collective_id=0, has_side_effects=True, vmem_limit_bytes=40 * 2**20

time: 123 us -> 102 us (0.83)
  Pallas kernels: 117 us -> 96 us
    pallas_call x1, Pallas kernels: 117 us -> 96 us  [local(): pl.pallas_call(body, out_shape=(jax.ShapeDtypeStruct(matrix.shape, F32),...]
where the time goes in v2:
time: 102 us
  Pallas kernels  96 us (94%)
  local copies, waits for them, and re-layouts  5.61 us (6%)
    pallas_call x1, Pallas kernels, local(): pl.pallas_call(body, out_shape=(jax.ShapeDtypeStruct(matrix.shape, F32),...  96 us
    unnamed x6, local copies, waits for them, and re-layouts  5.1 us

profile of v2, /device:TPU:1, one launch (start us, length us, event | category | flops | bytes accessed | tf_op | source)
XLA Modules:
  0.0 102.3 jit_solution(3163560141292661562)
XLA Ops:
  0.6 0.0 copy-start
  0.6 1.6 %copy-done = f32[2048,256]{1,0:T(8,128)S(1)} copy-done((f32[2048,256]{1,0:T(8,128)S(1)}, f32[2048,256]{1,0:T(8,128)}, u32[]{:S(2)}) %copy-start) | copy-done | bytes 2097176
  2.2 0.0 copy-start.1
  2.2 1.2 %copy-done.1 = f32[1024,256]{1,0:T(8,128)S(1)} copy-done((f32[1024,256]{1,0:T(8,128)S(1)}, f32[1024,256]{1,0:T(8,128)}, u32[]{:S(2)}) %copy-start.1) | copy-done | bytes 1048600
  3.4 96.0 %shard_map.49 = (f32[2048,256]{1,0:T(8,128)S(1)}, f32[1024,256]{1,0:T(8,128)S(1)}, f32[8,128]{1,0:T(8,128)S(1)}) custom-call(f32[2048,256]{1,0:T(8,128)S(1)} %copy-done, f32[1024,256]{1,0:T(8,128)S(1)} %copy-done.1), custom_call_target="tpu_custom_call" | custom-call | tf_op jit(solution)/shard_map/pallas_call | solution.py:508
  99.5 0.5 slice_bitcast_fusion
  100.0 1.3 %copy.7 = f32[2048,256]{1,0:T(8,128)} copy(f32[2048,256]{1,0:T(8,128)S(1)} %get-tuple-element.12) | data formatting | bytes 4194304
  101.3 1.0 copy.8
Async XLA Ops:
  0.6 1.6 %copy-start = (f32[2048,256]{1,0:T(8,128)S(1)}, f32[2048,256]{1,0:T(8,128)}, u32[]{:S(2)}) copy-start(f32[2048,256]{1,0:T(8,128)} %a_ref.1) | copy-start | bytes 6291460
  2.2 1.2 %copy-start.1 = (f32[1024,256]{1,0:T(8,128)S(1)}, f32[1024,256]{1,0:T(8,128)}, u32[]{:S(2)}) copy-start(f32[1024,256]{1,0:T(8,128)} %v_ref.1) | copy-start | bytes 3145732

commit v3 on v2

--- a/solution.py
+++ b/solution.py
@@ -18,7 +18,7 @@
 SMALL = 128
 RAW = 3
 RAW_FIRST = 128
-EARLY = 1
+EARLY = 2
 MIDDLE = 1
 CORRECT = 1
 
@@ -139,7 +139,7 @@
     a_ref, v_ref, ao_ref, vo_ref, m_ref,
     held, sent, got, done, raw, relayed, s, splat, hh, hl, qh, ql, ph, pl_, q_out, q_in,
     part, near, half, far, full, mine, groups,
-    in_sem, up_s, up_r, dn_s, dn_r, raw_s, raw_r, rel_s, rel_r, turn_s, turn_r, sum_s, sum_r, grp_s, grp_r, out_sem,
+    answer, group_answer, in_sem, up_s, up_r, dn_s, dn_r, raw_s, raw_r, rel_s, rel_r, turn_s, turn_r, sum_s, sum_r, grp_s, grp_r, out_sem,
 ):
     rows_a, rows_v = a_ref.shape[0], v_ref.shape[0]
     chunks_a, small = rows_a // CHUNK, rows_v // SMALL
@@ -153,16 +153,28 @@
     mate = p + 1 - 2 * odd
     to = p + 2 - 4 * odd
     source = p - 2 + 4 * odd
+    beyond = p - 1 + 2 * odd
     pa, pb = p // inner, lax.rem(p, inner)
+    halves_z = 2 - outer % 2
+    count_y = outer // halves_z
+    pm = lax.rem(pa, halves_z) * count_y + pa // halves_z
+    line = inner * halves_z
     up_from = (pairs - p) // pairs
     has_up, has_dn = p < pairs - 1, p > 0
     has_to = (to >= 0) & (to < pairs)
     has_source = (source >= 0) & (source < pairs)
+    has_beyond = (beyond >= 0) & (beyond < pairs)
+    last_of_line = (lax.rem(p, line) == line - 1) & (p < pairs - 1)
 
     def group_device(stage, other):
-        return (pa * inner + other, r) if stage == 0 else (other * inner + pb, r)
-
-    sizes, place = (inner, outer), (pb, pa)
+        if stage == 0:
+            return (pa * inner + other, r)
+        return ((lax.rem(other, count_y) * halves_z + other // count_y) * inner + pb, r)
+
+    sizes, place = (inner, outer), (pb, pm)
+
+    def later(other):
+        return (other > p) == (other // line == p // line)
 
     def remote(src, dst, send_sem, recv_sem, device):
         return pltpu.make_async_remote_copy(
@@ -176,20 +188,54 @@
 
     hello((p, beside))
     hello((p, across))
-    for stage in range(2):
-        for k in range(1, sizes[stage]):
-            hello(group_device(stage, lax.rem(place[stage] + k, sizes[stage])))
-
-    for there, device in ((has_up, p + 1), (has_dn, p - 1), (has_to, to), (has_source, source)):
-
-        @pl.when(there)
+    hello((mate, r))
+    others = ((has_beyond, beyond, 0), (has_to, to, 2), (has_source, source, 1))
+    for there, device, _ in others:
+
+        @pl.when(there & later(device))
         def _(device=device):
             hello((device, r))
 
+    def group_peers():
+        for stage in range(2):
+            for k in range(1, sizes[stage]):
+                yield stage, lax.rem(place[stage] + k, sizes[stage])
+
+    for stage, other in group_peers():
+
+        @pl.when(other > place[stage])
+        def _(stage=stage, other=other):
+            hello(group_device(stage, other))
+
     def barrier():
-        ends = up_from + (p + 1) // pairs
-        ends = ends + (pairs + 1 - p) // pairs + (p + 2) // pairs
-        pl.semaphore_wait(bar, 2 + inner - 1 + outer - 1 + 4 - ends)
+        count = 3 + pb + pm
+        for there, device, _ in others:
+            count = count + jnp.where(there & jnp.logical_not(later(device)), 1, 0)
+        pl.semaphore_wait(bar, count)
+        for there, device, which in others:
+
+            @pl.when(there & jnp.logical_not(later(device)))
+            def _(device=device, which=which):
+                pl.semaphore_signal(answer.at[which], 1, device_id=(device, r), device_id_type=MESH)
+
+        for stage, other in group_peers():
+
+            @pl.when(other < place[stage])
+            def _(stage=stage, other=other):
+                device = group_device(stage, other)
+                pl.semaphore_signal(group_answer.at[stage], 1, device_id=device, device_id_type=MESH)
+
+    def answered(which):
+        there, device, _ = others[which]
+
+        @pl.when(there & later(device))
+        def _():
+            pl.semaphore_wait(answer.at[which], 1)
+
+    def group_answered(stage):
+        @pl.when(place[stage] < sizes[stage] - 1)
+        def _():
+            pl.semaphore_wait(group_answer.at[stage], sizes[stage] - 1 - place[stage])
 
     def rows(c, size=CHUNK):
         return pl.ds(pl.multiple_of(c * size, size), size)
@@ -286,14 +332,31 @@
             return remote(q_out.at[core], q_in.at[core], turn_s.at[0], turn_r.at[0], (mate, r))
         return remote(q_in.at[core], q_in.at[core], turn_s.at[1], turn_r.at[1], (p, beside))
 
-    def send(c):
+    def send_up(c):
         @pl.when(has_up)
         def _():
             up(c).start()
 
+    def send_down(c):
         @pl.when(has_dn)
         def _():
             down(c).start()
+
+    def send_all(lo, hi, make, before=lambda c: None):
+        @pl.loop(lo, hi)
+        def _(c):
+            before(c)
+            send_up(make(c))
+
+            @pl.when(jnp.logical_not(last_of_line))
+            def _():
+                send_down(make(c))
+
+        @pl.when(last_of_line)
+        def _():
+            @pl.loop(lo, hi)
+            def _(c):
+                send_down(make(c))
 
     def receive(c):
         @pl.when(has_dn)
@@ -329,6 +392,7 @@
         return remote(mine.at[stage], dst, grp_s.at[stage, k], grp_r.at[stage, here], group_device(stage, other))
 
     def group_send(stage, value):
+        group_answered(stage)
         mine[stage] = value
         groups[stage, place[stage]] = value
         for k in range(1, sizes[stage]):
@@ -364,10 +428,8 @@
     q_out[1] = turn[BLK:]
     turn_copy(0).start()
 
-    @pl.loop(RAW, chunks_a)
-    def _(c):
-        turn_rows(rows(c))
-        send(chunk(c))
+    answered(0)
+    send_all(RAW, chunks_a, chunk, lambda c: turn_rows(rows(c)))
 
     turn_copy(0).wait_recv()
     turn_copy(1).start()
@@ -379,6 +441,8 @@
 
     raw_copy(0).wait_recv()
     raw_copy(1).wait_recv()
+    answered(1)
+    answered(2)
 
     @pl.loop(0, RAW)
     def _(c):
@@ -401,8 +465,7 @@
     def _(c):
         turn_rows(pl.ds(pl.multiple_of(rows_a + c * PIECE, PIECE), PIECE))
 
-    for v in range(EARLY):
-        send(small_chunk(v))
+    send_all(0, EARLY, small_chunk)
 
     clear_gram()
 
@@ -420,8 +483,7 @@
         add_gram(arrived(rows(c)))
 
     def some_vectors():
-        for v in range(EARLY, EARLY + MIDDLE):
-            send(small_chunk(v))
+        send_all(EARLY, EARLY + MIDDLE, small_chunk)
 
     gram = sum_over_row(1, some_vectors)
     mass_two = off_mass(gram)
@@ -429,9 +491,7 @@
     both = jnp.where(first, jnp.broadcast_to(mass_one, (8, 128)), jnp.broadcast_to(mass_two, (8, 128)))
     group_send(0, both)
 
-    @pl.loop(EARLY + MIDDLE, small)
-    def _(v):
-        send(small_chunk(v))
+    send_all(EARLY + MIDDLE, small, small_chunk)
 
     take_turn(gram)
     group_send(1, group_sum(0))
@@ -542,6 +602,8 @@
             vmem((2, 2, 192, 128), F32),
             vmem((2, 8, 128), F32),
             vmem((2, 8, 8, 128), F32),
+            pltpu.SemaphoreType.REGULAR((3,)),
+            pltpu.SemaphoreType.REGULAR((2,)),
             dma((rows_a // PIECE + 1,)),
             dma((sends,)),
             dma((sends,)),

time: 102 us -> 96 us (0.941)
  Pallas kernels: 96 us -> 89.6 us
    pallas_call x1, Pallas kernels: 96 us -> 89.6 us  [local(): pl.pallas_call(body, out_shape=(jax.ShapeDtypeStruct(matrix.shape, F32),...]
where the time goes in v3:
time: 96 us; the launch traced here: 95.9 us
  Pallas kernels  89.6 us (93%)
  local copies, waits for them, and re-layouts  5.61 us (6%)
    pallas_call x1, Pallas kernels, local(): pl.pallas_call(body, out_shape=(jax.ShapeDtypeStruct(matrix.shape, F32),...  89.6 us
    unnamed x6, local copies, waits for them, and re-layouts  5.1 us

profile of v3, /device:TPU:1, one launch (start us, length us, event | category | flops | bytes accessed | tf_op | source)
XLA Modules:
  0.0 95.9 jit_solution(12776942666360898132)
XLA Ops:
  0.6 0.0 copy-start
  0.6 1.6 %copy-done = f32[2048,256]{1,0:T(8,128)S(1)} copy-done((f32[2048,256]{1,0:T(8,128)S(1)}, f32[2048,256]{1,0:T(8,128)}, u32[]{:S(2)}) %copy-start) | copy-done | bytes 2097176
  2.2 0.0 copy-start.1
  2.2 1.2 %copy-done.1 = f32[1024,256]{1,0:T(8,128)S(1)} copy-done((f32[1024,256]{1,0:T(8,128)S(1)}, f32[1024,256]{1,0:T(8,128)}, u32[]{:S(2)}) %copy-start.1) | copy-done | bytes 1048600
  3.4 89.6 %shard_map.49 = (f32[2048,256]{1,0:T(8,128)S(1)}, f32[1024,256]{1,0:T(8,128)S(1)}, f32[8,128]{1,0:T(8,128)S(1)}) custom-call(f32[2048,256]{1,0:T(8,128)S(1)} %copy-done, f32[1024,256]{1,0:T(8,128)S(1)} %copy-done.1), custom_call_target="tpu_custom_call" | custom-call | tf_op jit(solution)/shard_map/pallas_call | solution.py:568
  93.1 0.5 slice_bitcast_fusion
  93.6 1.3 %copy.7 = f32[2048,256]{1,0:T(8,128)} copy(f32[2048,256]{1,0:T(8,128)S(1)} %get-tuple-element.12) | data formatting | bytes 4194304
  94.9 1.0 %copy.8 = f32[1024,256]{1,0:T(8,128)} copy(f32[1024,256]{1,0:T(8,128)S(1)} %get-tuple-element.13) | data formatting | bytes 2097152
Async XLA Ops:
  0.6 1.6 %copy-start = (f32[2048,256]{1,0:T(8,128)S(1)}, f32[2048,256]{1,0:T(8,128)}, u32[]{:S(2)}) copy-start(f32[2048,256]{1,0:T(8,128)} %a_ref.1) | copy-start | bytes 6291460
  2.2 1.2 %copy-start.1 = (f32[1024,256]{1,0:T(8,128)S(1)}, f32[1024,256]{1,0:T(8,128)}, u32[]{:S(2)}) copy-start(f32[1024,256]{1,0:T(8,128)} %v_ref.1) | copy-start | bytes 3145732

commit v4 on v3

--- a/solution.py
+++ b/solution.py
@@ -622,7 +622,7 @@
             dma((rows_a // PIECE + rows_v // SMALL,)),
         ],
         compiler_params=pltpu.CompilerParams(
-            collective_id=0, has_side_effects=True, vmem_limit_bytes=40 * 2**20
+            collective_id=0, has_side_effects=True, vmem_limit_bytes=48 * 2**20
         ),
     )(matrix, vectors)
     return matrix_out, vectors_out, mass[0, :2]

time: 96 us -> 95.2 us (level)
  local copies, waits for them, and re-layouts: 5.61 us -> 4.02 us
    unnamed x6 -> x4, local copies, waits for them, and re-layouts: 5.1 us -> 3.51 us
where the time goes in v4:
time: 95.2 us; the launch traced here: 95.1 us
  Pallas kernels  90.4 us (95%)
  local copies, waits for them, and re-layouts  4.02 us (4%)
    pallas_call x1, Pallas kernels, local(): pl.pallas_call(body, out_shape=(jax.ShapeDtypeStruct(matrix.shape, F32),...  90.4 us
    unnamed x4, local copies, waits for them, and re-layouts  3.51 us

profile of v4, /device:TPU:1, one launch (start us, length us, event | category | flops | bytes accessed | tf_op | source)
XLA Modules:
  0.0 95.1 jit_solution(1106743341959020879)
XLA Ops:
  0.6 0.0 copy-start
  0.6 1.2 %copy-done = f32[1024,256]{1,0:T(8,128)S(1)} copy-done((f32[1024,256]{1,0:T(8,128)S(1)}, f32[1024,256]{1,0:T(8,128)}, u32[]{:S(2)}) %copy-start) | copy-done | bytes 1048600
  1.9 90.4 %shard_map.49 = (f32[2048,256]{1,0:T(8,128)S(1)}, f32[1024,256]{1,0:T(8,128)S(1)}, f32[8,128]{1,0:T(8,128)S(1)}) custom-call(f32[2048,256]{1,0:T(8,128)} %a_ref.1, f32[1024,256]{1,0:T(8,128)S(1)} %copy-done), custom_call_target="tpu_custom_call" | custom-call | tf_op jit(solution)/shard_map/pallas_call | solution.py:568
  92.3 0.5 slice_bitcast_fusion
  92.8 1.3 %copy.7 = f32[2048,256]{1,0:T(8,128)} copy(f32[2048,256]{1,0:T(8,128)S(1)} %get-tuple-element.12) | data formatting | bytes 4194304
  94.1 1.0 %copy.8 = f32[1024,256]{1,0:T(8,128)} copy(f32[1024,256]{1,0:T(8,128)S(1)} %get-tuple-element.13) | data formatting | bytes 2097152
Async XLA Ops:
  0.6 1.2 %copy-start = (f32[1024,256]{1,0:T(8,128)S(1)}, f32[1024,256]{1,0:T(8,128)}, u32[]{:S(2)}) copy-start(f32[1024,256]{1,0:T(8,128)} %v_ref.1) | copy-start | bytes 3145732

commit v5 on v4

--- a/solution.py
+++ b/solution.py
@@ -20,7 +20,6 @@
 RAW_FIRST = 128
 EARLY = 2
 MIDDLE = 1
-CORRECT = 1
 
 
 def dot(a, b, ca, cb):
@@ -127,10 +126,10 @@
     row = lax.broadcasted_iota(jnp.int32, (WIDE, WIDE), 0)
     col = lax.broadcasted_iota(jnp.int32, (WIDE, WIDE), 1)
     turn = dot(square, jnp.where(row >= col, s[...], 0.0), 1, 1)
-    for _ in range(CORRECT):
-        over = dot(turn, turn, 0, 0)
+    for product in (dot3, dot):
+        over = product(turn, turn, 0, 0)
         over = jnp.where(row == col, (over - 1.0) * 0.5, jnp.where(row < col, over, 0.0))
-        turn = turn - dot(turn, over, 1, 0)
+        turn = turn - dot3(turn, over, 1, 0)
     return turn
 
 

time: 95.2 us -> 96 us (level)
  no operation moved by 1% of the time
where the time goes in v5:
time: 96 us; the launch traced here: 95.8 us
  Pallas kernels  91.2 us (95%)
  local copies, waits for them, and re-layouts  4.02 us (4%)
    pallas_call x1, Pallas kernels, local(): pl.pallas_call(body, out_shape=(jax.ShapeDtypeStruct(matrix.shape, F32),...  91.2 us
    unnamed x4, local copies, waits for them, and re-layouts  3.51 us

profile of v5, /device:TPU:1, one launch (start us, length us, event | category | flops | bytes accessed | tf_op | source)
XLA Modules:
  0.0 95.8 jit_solution(13583129386982333375)
XLA Ops:
  0.6 0.0 copy-start
  0.6 1.2 %copy-done = f32[1024,256]{1,0:T(8,128)S(1)} copy-done((f32[1024,256]{1,0:T(8,128)S(1)}, f32[1024,256]{1,0:T(8,128)}, u32[]{:S(2)}) %copy-start) | copy-done | bytes 1048600
  1.9 91.2 %shard_map.49 = (f32[2048,256]{1,0:T(8,128)S(1)}, f32[1024,256]{1,0:T(8,128)S(1)}, f32[8,128]{1,0:T(8,128)S(1)}) custom-call(f32[2048,256]{1,0:T(8,128)} %a_ref.1, f32[1024,256]{1,0:T(8,128)S(1)} %copy-done), custom_call_target="tpu_custom_call" | custom-call | tf_op jit(solution)/shard_map/pallas_call | solution.py:567
  93.0 0.5 slice_bitcast_fusion
  93.5 1.3 %copy.7 = f32[2048,256]{1,0:T(8,128)} copy(f32[2048,256]{1,0:T(8,128)S(1)} %get-tuple-element.12) | data formatting | bytes 4194304
  94.9 1.0 %copy.8 = f32[1024,256]{1,0:T(8,128)} copy(f32[1024,256]{1,0:T(8,128)S(1)} %get-tuple-element.13) | data formatting | bytes 2097152
Async XLA Ops:
  0.6 1.2 %copy-start = (f32[1024,256]{1,0:T(8,128)S(1)}, f32[1024,256]{1,0:T(8,128)}, u32[]{:S(2)}) copy-start(f32[1024,256]{1,0:T(8,128)} %v_ref.1) | copy-start | bytes 3145732
